TPU v7x, 32 devices: a whole 2x2x4 slice. The times are simulated.
32 devices in a mesh: rep: 2 (over y), seq: 4 (over z), head: 2 (over x), sub: 2 (over core).
Axes of the slice: x: 2, y: 2, z: 4, core: 2. Of those that a mesh axis runs over, the one named last changes fastest.
Arguments:
- queries: bfloat16 [4096, 2048], P(('rep', 'seq', 'sub'), 'head'), parts along dimension 0, may hold values from -1.5 to 1.5
- key_vectors: bfloat16 [4096, 2048], P(('rep', 'seq'), 'head'), parts along dimension 0, may hold values from -1.5 to 1.5
- value_vectors: bfloat16 [4096, 2048], P(('rep', 'seq'), 'head'), parts along dimension 0, may hold values from -6 to 6
- gate_bins: int32 [4096, 16], P(('rep', 'seq'), 'head'), parts along dimension 0, may hold values from 0 to 2048
- doc_lengths: int32 [6], P('rep'), parts along dimension 0, may hold values from 1 to 1536, as said below
- decay_rates: float32 [16], P('head'), may hold values from 0.15 to 86
- ridge_terms: float32 [16], P('head'), may hold values from 0.5 to 2
Outputs:
- mesa_output: bfloat16 [4096, 2048], P(('rep', 'seq', 'sub'), 'head'), parts along dimension 0
There are 2 independent parts, one for each index of `rep`. A program takes and returns all parts, laid end to end along the dimension named above; an argument that names none is the same for every part. Nothing has to cross between parts.
Inputs may be any that keep to these rules, and one draw needn't show every extreme that they name: `doc_lengths`: the lengths sum to 2048.
All inputs are finite; a program needn't handle non-finite values.
Results may differ from a plain program's by a relative error of at most 0.001.
Values sent between devices are 32-bit elements; how exact they have to be, the bound alone decides.
A program may use at most 64 MiB of HBM per device.

v0:
```python
import functools

import jax
import jax.numpy as jnp
from jax import lax
from jax.experimental import pallas as pl
from jax.experimental.pallas import tpu as pltpu
from jax.sharding import PartitionSpec as P

ITERS = 4
GUARD = 1e-06
FAR = 1e30
MESH = pl.DeviceIdType.MESH
f32 = jnp.float32
bf16 = jnp.bfloat16


def mm(a, b):
    return jnp.dot(a, b, preferred_element_type=f32)


def mm_t(a, b):
    return lax.dot_general(a, b, (((0,), (0,)), ((), ())), preferred_element_type=f32)


def split(x):
    hi = x.astype(bf16)
    return hi, (x - hi.astype(f32)).astype(bf16)


def kernel(
    seq_size, heads, rows, total_tokens,
    lengths_ref, rates_ref, ridge_ref, q_ref, k_ref, v_ref, bins_ref, out_ref,
    bcol, brow, penalty, gram_in, mem_in, gram_out, mem_out,
    sent_g, sent_m, got_g, got_m, pass_sg, pass_sm, pass_rg, pass_rm,
):
    shard = k_ref.shape[0]
    half = heads // 2
    width = 128
    me = lax.axis_index("seq")
    core = lax.axis_index("sub")
    row_start = pl.multiple_of(core * rows, rows)
    first = me * shard
    has_prev = me > 0
    has_next = me < seq_size - 1

    barrier = pltpu.get_barrier_semaphore()
    pl.semaphore_signal(barrier, inc=1, device_id={"sub": 1 - core}, device_id_type=MESH)

    @pl.when(has_prev)
    def _():
        pl.semaphore_signal(barrier, inc=1, device_id={"seq": me - 1}, device_id_type=MESH)

    @pl.when(has_next)
    def _():
        pl.semaphore_signal(barrier, inc=1, device_id={"seq": me + 1}, device_id_type=MESH)

    bins = bins_ref[...]
    high = (bins >> 7).astype(f32).astype(bf16)
    low = (bins & 127).astype(f32).astype(bf16)
    key_i = lax.broadcasted_iota(jnp.int32, (shard, shard), 0)
    key_j = lax.broadcasted_iota(jnp.int32, (shard, shard), 1)
    lower = jnp.where(key_i >= key_j, 1.0, 0.0).astype(bf16)
    upper = jnp.where(key_i <= key_j, 1.0, 0.0).astype(bf16)
    bcol[...] = 128.0 * mm(lower, high) + mm(lower, low)
    brow[...] = 128.0 * mm_t(high, upper) + mm_t(low, upper)

    starts = []
    start = jnp.int32(0)
    for d in range(lengths_ref.shape[0]):
        starts.append(start)
        start = start + lengths_ref[d]

    def doc_of(pos):
        count = jnp.zeros_like(pos)
        for s in starts:
            count = count + jnp.where(pos >= s, 1, 0)
        return count

    key_pos = lax.broadcasted_iota(jnp.int32, (1, shard), 1)
    key_doc = doc_of(first + key_pos)
    query_doc = doc_of(first + row_start + lax.broadcasted_iota(jnp.int32, (1, rows), 1))
    column_doc = doc_of(first + row_start + lax.broadcasted_iota(jnp.int32, (rows, 1), 0))
    one = jnp.zeros((1, 1), jnp.int32)
    prior_doc = doc_of(one + (first - 1))
    before_doc = doc_of(one + (first + row_start - 1))
    end_doc = doc_of(one + (first + shard - 1))
    si = lax.broadcasted_iota(jnp.int32, (rows, rows), 0)
    ti = lax.broadcasted_iota(jnp.int32, (rows, rows), 1)
    penalty[...] = jnp.where((si <= ti) & (column_doc == query_doc), 0.0, FAR)
    end_keep = jnp.where(key_doc == end_doc, 1.0, 0.0)
    shard_keep = jnp.where(end_doc == prior_doc, 1.0, 0.0)
    early_keep = jnp.where(
        (key_doc[:, :rows] == before_doc) & (key_pos[:, :rows] < row_start), 1.0, 0.0
    )
    start_keep = jnp.where(before_doc == prior_doc, 1.0, 0.0)
    carried_keep = jnp.where(query_doc == before_doc, 1.0, 0.0)
    later_core = jnp.where(one + core > 0, 1.0, 0.0)

    def rate_of(h):
        return rates_ref[h] * (-1.0 / total_tokens)

    def lanes(h):
        return pl.ds(pl.multiple_of(h * width, width), width)

    def chain_decay(h):
        return shard_keep * jnp.exp(rate_of(h) * brow[pl.ds(h, 1), :][:, shard - 1 :])

    def own_sums(i, carry):
        h = core * half + i
        sums = brow[pl.ds(h, 1), :]
        weight = end_keep * jnp.exp(rate_of(h) * (sums[:, shard - 1 : shard] - sums))
        keys = k_ref[:, lanes(h)]
        hi, lo = split(keys.T.astype(f32) * weight)
        both = jnp.concatenate([keys, v_ref[:, lanes(h)]], axis=1)
        total = mm(hi, both) + mm(lo, both)
        gram_out[i] = total[:, :width]
        mem_out[i] = total[:, width:]
        return carry

    lax.fori_loop(0, half, own_sums, 0)

    pl.semaphore_wait(
        barrier, 1 + jnp.where(has_prev, 1, 0) + jnp.where(has_next, 1, 0)
    )

    def forward(src, dst, sent, got, i):
        return pltpu.make_async_remote_copy(
            src_ref=src.at[i], dst_ref=dst.at[core * half + i],
            send_sem=sent.at[i], recv_sem=got.at[i],
            device_id={"seq": jnp.minimum(me + 1, seq_size - 1)}, device_id_type=MESH,
        )

    def across(buf, sent, got, i):
        h = core * half + i
        return pltpu.make_async_remote_copy(
            src_ref=buf.at[h], dst_ref=buf.at[h],
            send_sem=sent.at[i], recv_sem=got.at[i],
            device_id={"sub": 1 - core}, device_id_type=MESH,
        )

    def across_in(buf, sent, got, i):
        h = (1 - core) * half + i
        return pltpu.make_async_remote_copy(
            src_ref=buf.at[h], dst_ref=buf.at[h],
            send_sem=sent.at[i], recv_sem=got.at[i],
            device_id={"sub": 1 - core}, device_id_type=MESH,
        )

    def chain_step(src, buf, sent, got, pass_s, pass_r, i):
        h = core * half + i

        @pl.when(has_prev)
        def _():
            pltpu.make_async_remote_copy(
                src_ref=src.at[i], dst_ref=buf.at[h],
                send_sem=sent.at[i], recv_sem=got.at[i],
                device_id={"seq": jnp.maximum(me - 1, 0)}, device_id_type=MESH,
            ).wait_recv()
            across(buf, pass_s, pass_r, i).start()

            @pl.when(has_next)
            def _():
                src[i] = chain_decay(h) * buf[h] + src[i]

        @pl.when(has_next)
        def _():
            forward(src, buf, sent, got, i).start()

    def gram_step(i, carry):
        chain_step(gram_out, gram_in, sent_g, got_g, pass_sg, pass_rg, i)
        return carry

    @pl.when(jnp.logical_not(has_prev))
    def _():
        gram_in[...] = jnp.zeros_like(gram_in)
        mem_in[...] = jnp.zeros_like(mem_in)

    lax.fori_loop(0, half, gram_step, 0)

    head_lane = lax.broadcasted_iota(jnp.int32, (rows, heads), 1)

    def pair(i, carry):
        @pl.when(has_prev)
        def _():
            across_in(gram_in, pass_sg, pass_rg, i).wait_recv()

        group = (i, half + i)
        state = []
        for h in group:
            rate = rate_of(h)
            sums = brow[pl.ds(h, 1), :]
            query_sums = jnp.where(core > 0, sums[:, shard - rows :], sums[:, :rows])
            before = later_core * sums[:, rows - 1 : rows]
            column = jnp.sum(
                jnp.where(head_lane == h, bcol[pl.ds(row_start, rows), :], 0.0),
                axis=1, keepdims=True,
            )
            weights = jnp.exp(rate * (query_sums - column) - penalty[...])
            carried = carried_keep * jnp.exp(rate * (query_sums - before))
            decay = start_keep * jnp.exp(rate * before)
            early = early_keep * jnp.exp(
                rate * jnp.maximum(before - sums[:, :rows], 0.0)
            )
            old_keys = k_ref[0:rows, lanes(h)]
            hi, lo = split(old_keys.T.astype(f32) * early)
            both = jnp.concatenate([old_keys, v_ref[0:rows, lanes(h)]], axis=1)
            local = mm(hi, both) + mm(lo, both)
            ghi, glo = split(decay * gram_in[h] + local[:, :width])
            keys = k_ref[pl.ds(row_start, rows), lanes(h)]
            left = jnp.concatenate(
                [
                    jnp.concatenate([keys, keys], axis=1),
                    jnp.concatenate([ghi, ghi], axis=1),
                    jnp.concatenate([glo, glo], axis=1),
                ],
                axis=0,
            )
            query = q_ref[:, lanes(h)].T.astype(f32)
            state.append(
                dict(
                    weights=weights, carried=carried, decay=decay, mem=local[:, width:],
                    left=left, keys=keys, keys_t=keys.T, ridge=ridge_ref[h],
                    x=jnp.zeros_like(query), r=query, p=query,
                    energy=jnp.sum(query * query, axis=0, keepdims=True),
                )
            )
        for iteration in range(ITERS):
            for s in state:
                hi, lo = split(s["p"])
                s["y"] = mm(s["left"], jnp.concatenate([hi, lo], axis=0))
            for s in state:
                hi, lo = split(s["y"][:rows] * s["weights"])
                a = mm(s["keys_t"], hi) + mm(s["keys_t"], lo)
                earlier = s["y"][rows : rows + width] + s["y"][rows + width :]
                s["a"] = s["carried"] * earlier + a + s["ridge"] * s["p"]
            for s in state:
                p, a = s["p"], s["a"]
                alpha = s["energy"] / (jnp.sum(p * a, axis=0, keepdims=True) + GUARD)
                s["x"] = s["x"] + alpha * p
                if iteration < ITERS - 1:
                    r = s["r"] - alpha * a
                    energy = jnp.sum(r * r, axis=0, keepdims=True)
                    s["p"] = r + (energy / (s["energy"] + GUARD)) * p
                    s["r"], s["energy"] = r, energy

        chain_step(mem_out, mem_in, sent_m, got_m, pass_sm, pass_rm, i)
        within = []
        for h, s in zip(group, state):
            hi, lo = split(s["x"])
            s["hilo"] = jnp.concatenate([hi, lo], axis=0)
            keys2 = s["left"][:rows]
            hi, lo = split(mm(keys2, s["hilo"]) * s["weights"])
            values_t = v_ref[pl.ds(row_start, rows), lanes(h)].T
            within.append(mm(values_t, hi) + mm(values_t, lo))

        @pl.when(has_prev)
        def _():
            across_in(mem_in, pass_sm, pass_rm, i).wait_recv()

        for h, s, inner in zip(group, state, within):
            mhi, mlo = split((s["decay"] * mem_in[h] + s["mem"]).T)
            left = jnp.concatenate(
                [
                    jnp.concatenate([mhi, mhi], axis=1),
                    jnp.concatenate([mlo, mlo], axis=1),
                ],
                axis=0,
            )
            y = mm(left, s["hilo"])
            out = s["carried"] * (y[:width] + y[width:]) + inner
            out_ref[:, lanes(h)] = out.T.astype(bf16)
        return carry

    lax.fori_loop(0, half, pair, 0)

    def finish(i, carry):
        @pl.when(has_prev)
        def _():
            across(gram_in, pass_sg, pass_rg, i).wait_send()
            across(mem_in, pass_sm, pass_rm, i).wait_send()

        @pl.when(has_next)
        def _():
            forward(gram_out, gram_in, sent_g, got_g, i).wait_send()
            forward(mem_out, mem_in, sent_m, got_m, i).wait_send()

        return carry

    lax.fori_loop(0, half, finish, 0)


def per_device(seq_size, queries, keys, values, gate_bins, doc_lengths, decay_rates, ridge_terms):
    heads = decay_rates.shape[0]
    rows = queries.shape[0]
    shard = keys.shape[0]
    half = heads // 2
    width = keys.shape[1] // heads
    smem = pl.BlockSpec(memory_space=pltpu.SMEM)
    vmem = pl.BlockSpec(memory_space=pltpu.VMEM)
    flops = 2 * heads * rows * 256 * 768 * 5
    return pl.pallas_call(
        functools.partial(kernel, seq_size, heads, rows, shard * seq_size),
        out_shape=jax.ShapeDtypeStruct(queries.shape, bf16),
        in_specs=[smem, smem, smem, vmem, vmem, vmem, vmem],
        out_specs=vmem,
        scratch_shapes=[
            pltpu.VMEM((shard, heads), f32),
            pltpu.VMEM((heads, shard), f32),
            pltpu.VMEM((rows, rows), f32),
            pltpu.VMEM((heads, width, width), f32),
            pltpu.VMEM((heads, width, width), f32),
            pltpu.VMEM((half, width, width), f32),
            pltpu.VMEM((half, width, width), f32),
        ] + [pltpu.SemaphoreType.DMA((half,))] * 8,
        compiler_params=pltpu.CompilerParams(
            collective_id=0, has_side_effects=True, vmem_limit_bytes=48 * 1024 * 1024
        ),
        cost_estimate=pl.CostEstimate(
            flops=flops, bytes_accessed=4 * 1024 * 1024, transcendentals=heads * rows * rows
        ),
    )(doc_lengths, decay_rates, ridge_terms, queries, keys, values, gate_bins)


def solution(mesh):
    in_specs = (
        P(("rep", "seq", "sub"), "head"),
        P(("rep", "seq"), "head"),
        P(("rep", "seq"), "head"),
        P(("rep", "seq"), "head"),
        P("rep"),
        P("head"),
        P("head"),
    )
    out_specs = P(("rep", "seq", "sub"), "head")
    return jax.shard_map(
        functools.partial(per_device, mesh.shape["seq"]),
        mesh=mesh, in_specs=in_specs, out_specs=out_specs, check_vma=False,
    )
```

profile of v0, /device:TPU:31, one launch (start us, length us, event | category | flops | bytes accessed | tf_op | source)
XLA Modules:
  0.0 37.2 jit_solution(5941660103112776282)
XLA Ops:
  0.0 0.0 copy-start.5
  0.0 0.0 copy-start.4
  0.0 0.0 copy-start.3
  0.0 0.9 %copy.8.bins_ref = s32[512,8]{1,0:T(8,128)S(1)} copy(s32[512,8]{0,1:T(8,128)} %param.10) | data formatting | bytes 32768 | tf_op args[3]
  0.9 0.0 copy-done.5
  0.9 0.0 copy-done.4
  0.9 0.0 copy-done.3
  0.9 0.0 copy-start
  0.9 1.2 %copy-done = bf16[512,1024]{1,0:T(8,128)(2,1)S(1)} copy-done((bf16[512,1024]{1,0:T(8,128)(2,1)S(1)}, bf16[512,1024]{1,0:T(8,128)(2,1)}, u32[]{:S(2)}) %copy-start) | copy-done | bytes 1048600
  2.2 0.0 copy-start.1
  2.2 1.2 %copy-done.1 = bf16[512,1024]{1,0:T(8,128)(2,1)S(1)} copy-done((bf16[512,1024]{1,0:T(8,128)(2,1)S(1)}, bf16[512,1024]{1,0:T(8,128)(2,1)}, u32[]{:S(2)}) %copy-start.1) | copy-done | bytes 1048600
  3.4 0.0 copy-start.2
  3.4 1.0 %copy-done.2 = bf16[256,1024]{1,0:T(8,128)(2,1)S(1)} copy-done((bf16[256,1024]{1,0:T(8,128)(2,1)S(1)}, bf16[256,1024]{1,0:T(8,128)(2,1)}, u32[]{:S(2)}) %copy-start.2) | copy-done | bytes 524312
  4.4 32.0 %shard_map.73 = bf16[256,1024]{1,0:T(8,128)(2,1)S(1)} custom-call(s32[3]{0:T(128)S(1)} %copy-done.3, f32[8]{0:T(128)S(1)} %copy-done.4, f32[8]{0:T(128)S(1)} %copy-done.5, bf16[256,1024]{1,0:T(8,128)(2,1)S(1)} %copy-done.2, bf16[512,1024]{1,0:T(8,128)(2,1)S(1)} %copy-done, bf16[512,1024]{1,0:T(8,128)(2,1)S(1)} %copy-done.1, s32[512,8]{1,0:T(8,128)S(1)} %copy.8.bins_ref), custom_call_target="tpu_custom_call" | custom-call | flops 4026531840 | bytes 4194304 | tf_op jit(solution)/shard_map/pallas_call | solution.py:302
  36.4 0.8 %copy.10 = bf16[256,1024]{1,0:T(8,128)(2,1)} copy(bf16[256,1024]{1,0:T(8,128)(2,1)S(1)} %shard_map.73) | data formatting | bytes 1048576
Async XLA Ops:
  0.0 0.9 %copy-start.5 = (f32[8]{0:T(128)S(1)}, f32[8]{0:T(128)}, u32[]{:S(2)}) copy-start(f32[8]{0:T(128)} %ridge_ref.1) | copy-start | bytes 100
  0.0 0.9 %copy-start.4 = (f32[8]{0:T(128)S(1)}, f32[8]{0:T(128)}, u32[]{:S(2)}) copy-start(f32[8]{0:T(128)} %rates_ref.1) | copy-start | bytes 100
  0.0 0.9 %copy-start.3 = (s32[3]{0:T(128)S(1)}, s32[3]{0:T(128)}, u32[]{:S(2)}) copy-start(s32[3]{0:T(128)} %lengths_ref.1) | copy-start | bytes 40
  0.9 1.2 %copy-start = (bf16[512,1024]{1,0:T(8,128)(2,1)S(1)}, bf16[512,1024]{1,0:T(8,128)(2,1)}, u32[]{:S(2)}) copy-start(bf16[512,1024]{1,0:T(8,128)(2,1)} %k_ref.1) | copy-start | bytes 3145732
  2.2 1.2 %copy-start.1 = (bf16[512,1024]{1,0:T(8,128)(2,1)S(1)}, bf16[512,1024]{1,0:T(8,128)(2,1)}, u32[]{:S(2)}) copy-start(bf16[512,1024]{1,0:T(8,128)(2,1)} %v_ref.1) | copy-start | bytes 3145732
  3.4 1.0 %copy-start.2 = (bf16[256,1024]{1,0:T(8,128)(2,1)S(1)}, bf16[256,1024]{1,0:T(8,128)(2,1)}, u32[]{:S(2)}) copy-start(bf16[256,1024]{1,0:T(8,128)(2,1)} %q_ref.1) | copy-start | bytes 1572868
where the time goes:
time: 37.5 us; the launch traced here: 37.2 us
  Pallas kernels  32 us (85%)
  local copies, waits for them, and re-layouts  5.17 us (14%)
    pallas_call x1, Pallas kernels, per_device(): pl.pallas_call(functools.partial(kernel, seq_size, heads, rows, shard * s...  32 us
    unnamed x14, local copies, waits for them, and re-layouts  5.17 us

commit v1 on v0

--- a/solution.py
+++ b/solution.py
@@ -19,8 +19,8 @@
     return jnp.dot(a, b, preferred_element_type=f32)
 
 
-def mm_t(a, b):
-    return lax.dot_general(a, b, (((0,), (0,)), ((), ())), preferred_element_type=f32)
+def mm_nt(a, b):
+    return lax.dot_general(a, b, (((1,), (1,)), ((), ())), preferred_element_type=f32)
 
 
 def split(x):
@@ -30,9 +30,11 @@
 
 def kernel(
     seq_size, heads, rows, total_tokens,
-    lengths_ref, rates_ref, ridge_ref, q_ref, k_ref, v_ref, bins_ref, out_ref,
+    lengths_ref, rates_ref, ridge_ref, q_hbm, k_hbm, v_hbm, bins_hbm, out_ref,
+    q_ref, k_ref, v_ref, bins_ref,
     bcol, brow, penalty, gram_in, mem_in, gram_out, mem_out,
-    sent_g, sent_m, got_g, got_m, pass_sg, pass_sm, pass_rg, pass_rm,
+    weight_s, local_g, local_m, keys_ts, values_ts, query_ts,
+    sent_g, sent_m, got_g, got_m, pass_sg, pass_sm, pass_rg, pass_rm, load_sem,
 ):
     shard = k_ref.shape[0]
     half = heads // 2
@@ -44,6 +46,17 @@
     has_prev = me > 0
     has_next = me < seq_size - 1
 
+    loads = [(bins_hbm, bins_ref)]
+    piece = shard // 4
+    for src, dst in ((k_hbm, k_ref), (v_hbm, v_ref), (q_hbm, q_ref)):
+        for at in range(0, src.shape[0], piece):
+            loads.append((src.at[pl.ds(at, piece)], dst.at[pl.ds(at, piece)]))
+    loads = [
+        pltpu.make_async_copy(src, dst, load_sem.at[at]) for at, (src, dst) in enumerate(loads)
+    ]
+    for load in loads:
+        load.start()
+
     barrier = pltpu.get_barrier_semaphore()
     pl.semaphore_signal(barrier, inc=1, device_id={"sub": 1 - core}, device_id_type=MESH)
 
@@ -55,6 +68,7 @@
     def _():
         pl.semaphore_signal(barrier, inc=1, device_id={"seq": me + 1}, device_id_type=MESH)
 
+    loads[0].wait()
     bins = bins_ref[...]
     high = (bins >> 7).astype(f32).astype(bf16)
     low = (bins & 127).astype(f32).astype(bf16)
@@ -62,8 +76,8 @@
     key_j = lax.broadcasted_iota(jnp.int32, (shard, shard), 1)
     lower = jnp.where(key_i >= key_j, 1.0, 0.0).astype(bf16)
     upper = jnp.where(key_i <= key_j, 1.0, 0.0).astype(bf16)
-    bcol[...] = 128.0 * mm(lower, high) + mm(lower, low)
-    brow[...] = 128.0 * mm_t(high, upper) + mm_t(low, upper)
+    bcol[...] = 128.0 * mm_nt(lower, high) + mm_nt(lower, low)
+    brow[...] = 128.0 * mm(high, upper) + mm(low, upper)
 
     starts = []
     start = jnp.int32(0)
@@ -106,24 +120,6 @@
     def chain_decay(h):
         return shard_keep * jnp.exp(rate_of(h) * brow[pl.ds(h, 1), :][:, shard - 1 :])
 
-    def own_sums(i, carry):
-        h = core * half + i
-        sums = brow[pl.ds(h, 1), :]
-        weight = end_keep * jnp.exp(rate_of(h) * (sums[:, shard - 1 : shard] - sums))
-        keys = k_ref[:, lanes(h)]
-        hi, lo = split(keys.T.astype(f32) * weight)
-        both = jnp.concatenate([keys, v_ref[:, lanes(h)]], axis=1)
-        total = mm(hi, both) + mm(lo, both)
-        gram_out[i] = total[:, :width]
-        mem_out[i] = total[:, width:]
-        return carry
-
-    lax.fori_loop(0, half, own_sums, 0)
-
-    pl.semaphore_wait(
-        barrier, 1 + jnp.where(has_prev, 1, 0) + jnp.where(has_next, 1, 0)
-    )
-
     def forward(src, dst, sent, got, i):
         return pltpu.make_async_remote_copy(
             src_ref=src.at[i], dst_ref=dst.at[core * half + i],
@@ -147,6 +143,24 @@
             device_id={"sub": 1 - core}, device_id_type=MESH,
         )
 
+    def own_sums(i, carry):
+        h = core * half + i
+        sums = brow[pl.ds(h, 1), :]
+        weight = end_keep * jnp.exp(rate_of(h) * (sums[:, shard - 1 :] - sums))
+        keys = k_ref[:, lanes(h)]
+        hi, lo = split(keys.T.astype(f32) * weight)
+        both = jnp.concatenate([keys, v_ref[:, lanes(h)]], axis=1)
+        total = mm(hi, both) + mm(lo, both)
+        gram_out[i] = total[:, :width]
+        mem_out[i] = total[:, width:]
+
+        @pl.when(jnp.logical_not(has_prev) & has_next)
+        def _():
+            forward(gram_out, gram_in, sent_g, got_g, i).start()
+            forward(mem_out, mem_in, sent_m, got_m, i).start()
+
+        return carry
+
     def chain_step(src, buf, sent, got, pass_s, pass_r, i):
         h = core * half + i
 
@@ -157,30 +171,76 @@
                 send_sem=sent.at[i], recv_sem=got.at[i],
                 device_id={"seq": jnp.maximum(me - 1, 0)}, device_id_type=MESH,
             ).wait_recv()
-            across(buf, pass_s, pass_r, i).start()
 
             @pl.when(has_next)
             def _():
                 src[i] = chain_decay(h) * buf[h] + src[i]
-
-        @pl.when(has_next)
-        def _():
-            forward(src, buf, sent, got, i).start()
-
-    def gram_step(i, carry):
+                forward(src, buf, sent, got, i).start()
+
+            across(buf, pass_s, pass_r, i).start()
+
+    def gram_step(i):
         chain_step(gram_out, gram_in, sent_g, got_g, pass_sg, pass_rg, i)
-        return carry
+
+    def mem_step(i):
+        chain_step(mem_out, mem_in, sent_m, got_m, pass_sm, pass_rm, i)
 
     @pl.when(jnp.logical_not(has_prev))
     def _():
         gram_in[...] = jnp.zeros_like(gram_in)
         mem_in[...] = jnp.zeros_like(mem_in)
 
-    lax.fori_loop(0, half, gram_step, 0)
+    pl.semaphore_wait(
+        barrier, 1 + jnp.where(has_prev, 1, 0) + jnp.where(has_next, 1, 0)
+    )
+    for load in loads[1:]:
+        load.wait()
+    lax.fori_loop(0, half, own_sums, 0)
 
     head_lane = lax.broadcasted_iota(jnp.int32, (rows, heads), 1)
 
+    def query_sums_of(h):
+        sums = brow[pl.ds(h, 1), :]
+        query_sums = jnp.where(core > 0, sums[:, shard - rows :], sums[:, :rows])
+        before = later_core * sums[:, rows - 1 : rows]
+        return sums, query_sums, before
+
+    def prepare(i):
+        for h in (i, half + i):
+            rate = rate_of(h)
+            sums, query_sums, before = query_sums_of(h)
+            column = jnp.sum(
+                jnp.where(head_lane == h, bcol[pl.ds(row_start, rows), :], 0.0),
+                axis=1, keepdims=True,
+            )
+            weight_s[h] = jnp.exp(rate * (query_sums - column) - penalty[...])
+            early = early_keep * jnp.exp(
+                rate * jnp.maximum(before - sums[:, :rows], 0.0)
+            )
+            old_keys = k_ref[0:rows, lanes(h)]
+            hi, lo = split(old_keys.T.astype(f32) * early)
+            both = jnp.concatenate([old_keys, v_ref[0:rows, lanes(h)]], axis=1)
+            local = mm(hi, both) + mm(lo, both)
+            local_g[h] = local[:, :width]
+            local_m[h] = local[:, width:]
+            keys_ts[h] = k_ref[pl.ds(row_start, rows), lanes(h)].T
+            values_ts[h] = v_ref[pl.ds(row_start, rows), lanes(h)].T
+            query_ts[h] = q_ref[:, lanes(h)].T
+
+    ahead = jnp.minimum(half, me * 2)
+
+    def prepare_ahead(i, carry):
+        prepare(i)
+        return carry
+
+    lax.fori_loop(0, ahead, prepare_ahead, 0)
+    gram_step(0)
+
     def pair(i, carry):
+        @pl.when(i >= ahead)
+        def _():
+            prepare(i)
+
         @pl.when(has_prev)
         def _():
             across_in(gram_in, pass_sg, pass_rg, i).wait_recv()
@@ -189,24 +249,10 @@
         state = []
         for h in group:
             rate = rate_of(h)
-            sums = brow[pl.ds(h, 1), :]
-            query_sums = jnp.where(core > 0, sums[:, shard - rows :], sums[:, :rows])
-            before = later_core * sums[:, rows - 1 : rows]
-            column = jnp.sum(
-                jnp.where(head_lane == h, bcol[pl.ds(row_start, rows), :], 0.0),
-                axis=1, keepdims=True,
-            )
-            weights = jnp.exp(rate * (query_sums - column) - penalty[...])
+            sums, query_sums, before = query_sums_of(h)
             carried = carried_keep * jnp.exp(rate * (query_sums - before))
             decay = start_keep * jnp.exp(rate * before)
-            early = early_keep * jnp.exp(
-                rate * jnp.maximum(before - sums[:, :rows], 0.0)
-            )
-            old_keys = k_ref[0:rows, lanes(h)]
-            hi, lo = split(old_keys.T.astype(f32) * early)
-            both = jnp.concatenate([old_keys, v_ref[0:rows, lanes(h)]], axis=1)
-            local = mm(hi, both) + mm(lo, both)
-            ghi, glo = split(decay * gram_in[h] + local[:, :width])
+            ghi, glo = split(decay * gram_in[h] + local_g[h])
             keys = k_ref[pl.ds(row_start, rows), lanes(h)]
             left = jnp.concatenate(
                 [
@@ -216,11 +262,11 @@
                 ],
                 axis=0,
             )
-            query = q_ref[:, lanes(h)].T.astype(f32)
+            query = query_ts[h].astype(f32)
             state.append(
                 dict(
-                    weights=weights, carried=carried, decay=decay, mem=local[:, width:],
-                    left=left, keys=keys, keys_t=keys.T, ridge=ridge_ref[h],
+                    h=h, carried=carried, decay=decay,
+                    left=left, ridge=ridge_ref[h],
                     x=jnp.zeros_like(query), r=query, p=query,
                     energy=jnp.sum(query * query, axis=0, keepdims=True),
                 )
@@ -230,8 +276,8 @@
                 hi, lo = split(s["p"])
                 s["y"] = mm(s["left"], jnp.concatenate([hi, lo], axis=0))
             for s in state:
-                hi, lo = split(s["y"][:rows] * s["weights"])
-                a = mm(s["keys_t"], hi) + mm(s["keys_t"], lo)
+                hi, lo = split(s["y"][:rows] * weight_s[s["h"]])
+                a = mm(keys_ts[s["h"]], hi) + mm(keys_ts[s["h"]], lo)
                 earlier = s["y"][rows : rows + width] + s["y"][rows + width :]
                 s["a"] = s["carried"] * earlier + a + s["ridge"] * s["p"]
             for s in state:
@@ -243,23 +289,27 @@
                     energy = jnp.sum(r * r, axis=0, keepdims=True)
                     s["p"] = r + (energy / (s["energy"] + GUARD)) * p
                     s["r"], s["energy"] = r, energy
-
-        chain_step(mem_out, mem_in, sent_m, got_m, pass_sm, pass_rm, i)
+            if iteration == 1:
+                mem_step(i)
+
+        @pl.when(i < half - 1)
+        def _():
+            gram_step(i + 1)
+
         within = []
         for h, s in zip(group, state):
             hi, lo = split(s["x"])
             s["hilo"] = jnp.concatenate([hi, lo], axis=0)
             keys2 = s["left"][:rows]
-            hi, lo = split(mm(keys2, s["hilo"]) * s["weights"])
-            values_t = v_ref[pl.ds(row_start, rows), lanes(h)].T
-            within.append(mm(values_t, hi) + mm(values_t, lo))
+            hi, lo = split(mm(keys2, s["hilo"]) * weight_s[h])
+            within.append(mm(values_ts[h], hi) + mm(values_ts[h], lo))
 
         @pl.when(has_prev)
         def _():
             across_in(mem_in, pass_sm, pass_rm, i).wait_recv()
 
         for h, s, inner in zip(group, state, within):
-            mhi, mlo = split((s["decay"] * mem_in[h] + s["mem"]).T)
+            mhi, mlo = split((s["decay"] * mem_in[h] + local_m[h]).T)
             left = jnp.concatenate(
                 [
                     jnp.concatenate([mhi, mhi], axis=1),
@@ -298,28 +348,36 @@
     width = keys.shape[1] // heads
     smem = pl.BlockSpec(memory_space=pltpu.SMEM)
     vmem = pl.BlockSpec(memory_space=pltpu.VMEM)
+    hbm = pl.BlockSpec(memory_space=pltpu.HBM)
+    square = pltpu.VMEM((heads, width, width), f32)
+    turned = pltpu.VMEM((heads, width, rows), bf16)
     flops = 2 * heads * rows * 256 * 768 * 5
     return pl.pallas_call(
         functools.partial(kernel, seq_size, heads, rows, shard * seq_size),
         out_shape=jax.ShapeDtypeStruct(queries.shape, bf16),
-        in_specs=[smem, smem, smem, vmem, vmem, vmem, vmem],
+        in_specs=[smem, smem, smem, hbm, hbm, hbm, hbm],
         out_specs=vmem,
         scratch_shapes=[
+            pltpu.VMEM(queries.shape, bf16),
+            pltpu.VMEM(keys.shape, bf16),
+            pltpu.VMEM(values.shape, bf16),
+            pltpu.VMEM((heads, shard), jnp.int32),
             pltpu.VMEM((shard, heads), f32),
             pltpu.VMEM((heads, shard), f32),
             pltpu.VMEM((rows, rows), f32),
-            pltpu.VMEM((heads, width, width), f32),
-            pltpu.VMEM((heads, width, width), f32),
+            square, square,
             pltpu.VMEM((half, width, width), f32),
             pltpu.VMEM((half, width, width), f32),
-        ] + [pltpu.SemaphoreType.DMA((half,))] * 8,
+            pltpu.VMEM((heads, rows, rows), f32),
+            square, square, turned, turned, turned,
+        ] + [pltpu.SemaphoreType.DMA((half,))] * 8 + [pltpu.SemaphoreType.DMA((16,))],
         compiler_params=pltpu.CompilerParams(
-            collective_id=0, has_side_effects=True, vmem_limit_bytes=48 * 1024 * 1024
+            collective_id=0, has_side_effects=True, vmem_limit_bytes=62 * 1024 * 1024
         ),
         cost_estimate=pl.CostEstimate(
             flops=flops, bytes_accessed=4 * 1024 * 1024, transcendentals=heads * rows * rows
         ),
-    )(doc_lengths, decay_rates, ridge_terms, queries, keys, values, gate_bins)
+    )(doc_lengths, decay_rates, ridge_terms, queries, keys, values, gate_bins.T)
 
 
 def solution(mesh):

time: 37.5 us -> 30.6 us (0.82)
  Pallas kernels: 32 us -> 28.5 us
  local copies, waits for them, and re-layouts: 5.17 us -> 1.87 us
    pallas_call x1, Pallas kernels: 32 us -> 28.5 us  [per_device(): pl.pallas_call(functools.partial(kernel, seq_size, heads, rows, shard * s...]
    unnamed x14 -> x1, local copies, waits for them, and re-layouts: 5.17 us -> 1.87 us
where the time goes in v1:
time: 30.6 us; the launch traced here: 30.4 us
  Pallas kernels  28.5 us (93%)
  local copies, waits for them, and re-layouts  1.87 us (6%)
    pallas_call x1, Pallas kernels, per_device(): pl.pallas_call(functools.partial(kernel, seq_size, heads, rows, shard * s...  28.5 us
    unnamed x1, local copies, waits for them, and re-layouts  1.87 us

profile of v1, /device:TPU:31, one launch (start us, length us, event | category | flops | bytes accessed | tf_op | source)
XLA Modules:
  0.0 30.4 jit_solution(13139219768556238744)
XLA Ops:
  0.0 28.5 %shard_map.73 = bf16[256,1024]{1,0:T(8,128)(2,1)} custom-call(s32[3]{0:T(128)} %lengths_ref.1, f32[8]{0:T(128)} %rates_ref.1, f32[8]{0:T(128)} %ridge_ref.1, bf16[256,1024]{1,0:T(8,128)(2,1)} %q_hbm.1, bf16[512,1024]{1,0:T(8,128)(2,1)} %k_hbm.1, bf16[512,1024]{1,0:T(8,128)(2,1)} %v_hbm.1, s32[8,512]{1,0:T(8,128)} %bitcast.1), custom_call_target="tpu_custom_call" | custom-call | flops 4026531840 | bytes 4194304 | tf_op jit(solution)/shard_map/pallas_call | solution.py:355
  28.5 1.9 %copy.9 = bf16[256,1024]{1,0:T(8,128)(2,1)} copy(bf16[256,1024]{1,0:T(8,128)(2,1)} %shard_map.73) | data formatting | bytes 1048576

commit v2 on v1

--- a/solution.py
+++ b/solution.py
@@ -32,13 +32,14 @@
     seq_size, heads, rows, total_tokens,
     lengths_ref, rates_ref, ridge_ref, q_hbm, k_hbm, v_hbm, bins_hbm, out_ref,
     q_ref, k_ref, v_ref, bins_ref,
-    bcol, brow, penalty, gram_in, mem_in, gram_out, mem_out,
+    bcol, brow, penalty, came, flow,
     weight_s, local_g, local_m, keys_ts, values_ts, query_ts,
-    sent_g, sent_m, got_g, got_m, pass_sg, pass_sm, pass_rg, pass_rm, load_sem,
+    sent, got, pass_s, pass_r, load_sem,
 ):
     shard = k_ref.shape[0]
     half = heads // 2
-    width = 128
+    width = came.shape[3]
+    steps = flow.shape[0]
     me = lax.axis_index("seq")
     core = lax.axis_index("sub")
     row_start = pl.multiple_of(core * rows, rows)
@@ -143,7 +144,43 @@
             device_id={"sub": 1 - core}, device_id_type=MESH,
         )
 
-    def own_sums(i, carry):
+    wi = lax.broadcasted_iota(jnp.int32, (width, width), 0)
+    wj = lax.broadcasted_iota(jnp.int32, (width, width), 1)
+    upper_part = jnp.where(wi <= wj, 1, 0)
+    diagonal = wi == wj
+
+    def pieces(k):
+        end = width + 8 if k % 3 == 0 else width
+        return ((0, width // 2), (width // 2, end))
+
+    def forward(k, n):
+        low_row, high_row = pieces(k)[n]
+        at = pl.ds(low_row, high_row - low_row)
+        return pltpu.make_async_remote_copy(
+            src_ref=flow.at[k, at], dst_ref=came.at[core, k, at],
+            send_sem=sent.at[k, n], recv_sem=got.at[k, n],
+            device_id={"seq": jnp.minimum(me + 1, seq_size - 1)}, device_id_type=MESH,
+        )
+
+    def arrival(k, n):
+        low_row, high_row = pieces(k)[n]
+        at = pl.ds(low_row, high_row - low_row)
+        return pltpu.make_async_remote_copy(
+            src_ref=flow.at[k, at], dst_ref=came.at[core, k, at],
+            send_sem=sent.at[k, n], recv_sem=got.at[k, n],
+            device_id={"seq": jnp.maximum(me - 1, 0)}, device_id_type=MESH,
+        )
+
+    def across(owner, k, n):
+        low_row, high_row = pieces(k)[n]
+        at = pl.ds(low_row, high_row - low_row)
+        return pltpu.make_async_remote_copy(
+            src_ref=came.at[owner, k, at], dst_ref=came.at[owner, k, at],
+            send_sem=pass_s.at[k, n], recv_sem=pass_r.at[k, n],
+            device_id={"sub": 1 - core}, device_id_type=MESH,
+        )
+
+    def own_sums(i):
         h = core * half + i
         sums = brow[pl.ds(h, 1), :]
         weight = end_keep * jnp.exp(rate_of(h) * (sums[:, shard - 1 :] - sums))
@@ -151,51 +188,68 @@
         hi, lo = split(keys.T.astype(f32) * weight)
         both = jnp.concatenate([keys, v_ref[:, lanes(h)]], axis=1)
         total = mm(hi, both) + mm(lo, both)
-        gram_out[i] = total[:, :width]
-        mem_out[i] = total[:, width:]
-
+        k = 3 * (i // 2)
+        flow[k + 1 + i % 2, 0:width] = total[:, width:]
+        return total[:, :width]
+
+    def own_pair(p):
+        one_gram = own_sums(2 * p)
+        two_gram = own_sums(2 * p + 1)
+        flow[3 * p, 0:width] = jnp.where(wi <= wj, one_gram, two_gram)
+        flow[3 * p, width : width + 8] = jnp.broadcast_to(
+            jnp.sum(jnp.where(diagonal, two_gram, 0.0), axis=0, keepdims=True), (8, width)
+        )
+
+    def source_send(k):
         @pl.when(jnp.logical_not(has_prev) & has_next)
         def _():
-            forward(gram_out, gram_in, sent_g, got_g, i).start()
-            forward(mem_out, mem_in, sent_m, got_m, i).start()
-
-        return carry
-
-    def chain_step(src, buf, sent, got, pass_s, pass_r, i):
-        h = core * half + i
+            for n in range(2):
+                forward(k, n).start()
+
+    def chain_step(k):
+        h = core * half + 2 * (k // 3)
 
         @pl.when(has_prev)
         def _():
-            pltpu.make_async_remote_copy(
-                src_ref=src.at[i], dst_ref=buf.at[h],
-                send_sem=sent.at[i], recv_sem=got.at[i],
-                device_id={"seq": jnp.maximum(me - 1, 0)}, device_id_type=MESH,
-            ).wait_recv()
-
-            @pl.when(has_next)
-            def _():
-                src[i] = chain_decay(h) * buf[h] + src[i]
-                forward(src, buf, sent, got, i).start()
-
-            across(buf, pass_s, pass_r, i).start()
-
-    def gram_step(i):
-        chain_step(gram_out, gram_in, sent_g, got_g, pass_sg, pass_rg, i)
-
-    def mem_step(i):
-        chain_step(mem_out, mem_in, sent_m, got_m, pass_sm, pass_rm, i)
+            for n in range(2):
+                low_row, high_row = pieces(k)[n]
+                arrival(k, n).wait_recv()
+
+                @pl.when(has_next)
+                def _():
+                    if k % 3 == 0:
+                        one_decay, two_decay = chain_decay(h), chain_decay(h + 1)
+                        decay = jnp.where(
+                            wi[low_row:width] <= wj[low_row:width], one_decay, two_decay
+                        )
+                        decay = jnp.concatenate(
+                            [decay, jnp.broadcast_to(two_decay, (8, width))], axis=0
+                        )[: high_row - low_row]
+                    else:
+                        decay = chain_decay(h + k % 3 - 1)
+                    flow[k, low_row:high_row] = (
+                        decay * came[core, k, low_row:high_row] + flow[k, low_row:high_row]
+                    )
+                    forward(k, n).start()
+
+                across(core, k, n).start()
 
     @pl.when(jnp.logical_not(has_prev))
     def _():
-        gram_in[...] = jnp.zeros_like(gram_in)
-        mem_in[...] = jnp.zeros_like(mem_in)
-
+        came[...] = jnp.zeros_like(came)
+
+    for load in loads[1:9]:
+        load.wait()
+    own_pair(0)
     pl.semaphore_wait(
         barrier, 1 + jnp.where(has_prev, 1, 0) + jnp.where(has_next, 1, 0)
     )
-    for load in loads[1:]:
+    source_send(0)
+    for p in range(1, half // 2):
+        own_pair(p)
+    source_send(1)
+    for load in loads[9:]:
         load.wait()
-    lax.fori_loop(0, half, own_sums, 0)
 
     head_lane = lax.broadcasted_iota(jnp.int32, (rows, heads), 1)
 
@@ -234,25 +288,42 @@
         return carry
 
     lax.fori_loop(0, ahead, prepare_ahead, 0)
-    gram_step(0)
+    chain_step(0)
+
+    def await_other(k, when):
+        @pl.when(has_prev & when)
+        def _():
+            for n in range(2):
+                across(1 - core, k, n).wait_recv()
 
     def pair(i, carry):
+        parity = i % 2
+
         @pl.when(i >= ahead)
         def _():
             prepare(i)
 
-        @pl.when(has_prev)
-        def _():
-            across_in(gram_in, pass_sg, pass_rg, i).wait_recv()
+        def source_spot(spot):
+            for k in range(2, steps):
+                if (k - 2) % 3 == spot:
+                    pl.when(i == (k - 2) // 3)(functools.partial(source_send, k))
+
+        source_spot(0)
+        for k in range(0, steps, 3):
+            await_other(k, i == 2 * (k // 3))
 
         group = (i, half + i)
         state = []
-        for h in group:
+        for owner, h in enumerate(group):
             rate = rate_of(h)
             sums, query_sums, before = query_sums_of(h)
             carried = carried_keep * jnp.exp(rate * (query_sums - before))
             decay = start_keep * jnp.exp(rate * before)
-            ghi, glo = split(decay * gram_in[h] + local_g[h])
+            packed = came[owner, 3 * (i // 2)]
+            square = packed[:width]
+            gram = jnp.where(upper_part != parity, square, square.T)
+            gram = jnp.where(diagonal & (parity == 1), packed[width : width + 1], gram)
+            ghi, glo = split(decay * gram + local_g[h])
             keys = k_ref[pl.ds(row_start, rows), lanes(h)]
             left = jnp.concatenate(
                 [
@@ -289,12 +360,12 @@
                     energy = jnp.sum(r * r, axis=0, keepdims=True)
                     s["p"] = r + (energy / (s["energy"] + GUARD)) * p
                     s["r"], s["energy"] = r, energy
-            if iteration == 1:
-                mem_step(i)
-
-        @pl.when(i < half - 1)
-        def _():
-            gram_step(i + 1)
+            if iteration % 2 == 1:
+                spot = iteration // 2
+                source_spot(spot + 1)
+                for k in range(1, steps):
+                    if (k - 1) % 2 == spot:
+                        pl.when(i == (k - 1) // 2)(functools.partial(chain_step, k))
 
         within = []
         for h, s in zip(group, state):
@@ -304,12 +375,12 @@
             hi, lo = split(mm(keys2, s["hilo"]) * weight_s[h])
             within.append(mm(values_ts[h], hi) + mm(values_ts[h], lo))
 
-        @pl.when(has_prev)
-        def _():
-            across_in(mem_in, pass_sm, pass_rm, i).wait_recv()
-
-        for h, s, inner in zip(group, state, within):
-            mhi, mlo = split((s["decay"] * mem_in[h] + local_m[h]).T)
+        for k in range(steps):
+            if k % 3 > 0:
+                await_other(k, i == 2 * (k // 3) + k % 3 - 1)
+        for owner, (h, s, inner) in enumerate(zip(group, state, within)):
+            memory = came[owner, 3 * (i // 2) + 1 + parity][:width]
+            mhi, mlo = split((s["decay"] * memory + local_m[h]).T)
             left = jnp.concatenate(
                 [
                     jnp.concatenate([mhi, mhi], axis=1),
@@ -324,20 +395,17 @@
 
     lax.fori_loop(0, half, pair, 0)
 
-    def finish(i, carry):
-        @pl.when(has_prev)
-        def _():
-            across(gram_in, pass_sg, pass_rg, i).wait_send()
-            across(mem_in, pass_sm, pass_rm, i).wait_send()
-
-        @pl.when(has_next)
-        def _():
-            forward(gram_out, gram_in, sent_g, got_g, i).wait_send()
-            forward(mem_out, mem_in, sent_m, got_m, i).wait_send()
-
-        return carry
-
-    lax.fori_loop(0, half, finish, 0)
+    @pl.when(has_prev)
+    def _():
+        for k in range(steps):
+            for n in range(2):
+                across(core, k, n).wait_send()
+
+    @pl.when(has_next)
+    def _():
+        for k in range(steps):
+            for n in range(2):
+                forward(k, n).wait_send()
 
 
 def per_device(seq_size, queries, keys, values, gate_bins, doc_lengths, decay_rates, ridge_terms):
@@ -345,6 +413,7 @@
     rows = queries.shape[0]
     shard = keys.shape[0]
     half = heads // 2
+    steps = 3 * (half // 2)
     width = keys.shape[1] // heads
     smem = pl.BlockSpec(memory_space=pltpu.SMEM)
     vmem = pl.BlockSpec(memory_space=pltpu.VMEM)
@@ -365,12 +434,11 @@
             pltpu.VMEM((shard, heads), f32),
             pltpu.VMEM((heads, shard), f32),
             pltpu.VMEM((rows, rows), f32),
-            square, square,
-            pltpu.VMEM((half, width, width), f32),
-            pltpu.VMEM((half, width, width), f32),
+            pltpu.VMEM((2, steps, width + 8, width), f32),
+            pltpu.VMEM((steps, width + 8, width), f32),
             pltpu.VMEM((heads, rows, rows), f32),
             square, square, turned, turned, turned,
-        ] + [pltpu.SemaphoreType.DMA((half,))] * 8 + [pltpu.SemaphoreType.DMA((16,))],
+        ] + [pltpu.SemaphoreType.DMA((steps, 2))] * 4 + [pltpu.SemaphoreType.DMA((16,))],
         compiler_params=pltpu.CompilerParams(
             collective_id=0, has_side_effects=True, vmem_limit_bytes=62 * 1024 * 1024
         ),

time: 30.6 us -> 29.9 us (0.977)
  Pallas kernels: 28.5 us -> 27.8 us
    pallas_call x1, Pallas kernels: 28.5 us -> 27.8 us  [per_device(): pl.pallas_call(functools.partial(kernel, seq_size, heads, rows, shard * s...]
where the time goes in v2:
time: 29.9 us; the launch traced here: 29.7 us
  Pallas kernels  27.8 us (93%)
  local copies, waits for them, and re-layouts  1.87 us (6%)
    pallas_call x1, Pallas kernels, per_device(): pl.pallas_call(functools.partial(kernel, seq_size, heads, rows, shard * s...  27.8 us
    unnamed x1, local copies, waits for them, and re-layouts  1.87 us

profile of v2, /device:TPU:31, one launch (start us, length us, event | category | flops | bytes accessed | tf_op | source)
XLA Modules:
  0.0 29.7 jit_solution(2413152631110243251)
XLA Ops:
  0.0 27.8 %shard_map.73 = bf16[256,1024]{1,0:T(8,128)(2,1)} custom-call(s32[3]{0:T(128)} %lengths_ref.1, f32[8]{0:T(128)} %rates_ref.1, f32[8]{0:T(128)} %ridge_ref.1, bf16[256,1024]{1,0:T(8,128)(2,1)} %q_hbm.1, bf16[512,1024]{1,0:T(8,128)(2,1)} %k_hbm.1, bf16[512,1024]{1,0:T(8,128)(2,1)} %v_hbm.1, s32[8,512]{1,0:T(8,128)} %bitcast.1), custom_call_target="tpu_custom_call" | custom-call | flops 4026531840 | bytes 4194304 | tf_op jit(solution)/shard_map/pallas_call | solution.py:424
  27.8 1.9 %copy.9 = bf16[256,1024]{1,0:T(8,128)(2,1)} copy(bf16[256,1024]{1,0:T(8,128)(2,1)} %shard_map.73) | data formatting | bytes 1048576

commit v3 on v2

--- a/solution.py
+++ b/solution.py
@@ -361,11 +361,17 @@
                     s["p"] = r + (energy / (s["energy"] + GUARD)) * p
                     s["r"], s["energy"] = r, energy
             if iteration % 2 == 1:
-                spot = iteration // 2
-                source_spot(spot + 1)
-                for k in range(1, steps):
-                    if (k - 1) % 2 == spot:
-                        pl.when(i == (k - 1) // 2)(functools.partial(chain_step, k))
+                source_spot(iteration // 2 + 1)
+            for k in range(1, steps):
+                early_at, late_at = k - 1, 2 * k - 1
+                if early_at % ITERS == iteration:
+                    pl.when((i == early_at // ITERS) & has_next)(
+                        functools.partial(chain_step, k)
+                    )
+                if late_at % ITERS == iteration:
+                    pl.when((i == late_at // ITERS) & jnp.logical_not(has_next))(
+                        functools.partial(chain_step, k)
+                    )
 
         within = []
         for h, s in zip(group, state):
@@ -440,7 +446,7 @@
             square, square, turned, turned, turned,
         ] + [pltpu.SemaphoreType.DMA((steps, 2))] * 4 + [pltpu.SemaphoreType.DMA((16,))],
         compiler_params=pltpu.CompilerParams(
-            collective_id=0, has_side_effects=True, vmem_limit_bytes=62 * 1024 * 1024
+            collective_id=0, has_side_effects=True, vmem_limit_bytes=53 * 1024 * 1024
         ),
         cost_estimate=pl.CostEstimate(
             flops=flops, bytes_accessed=4 * 1024 * 1024, transcendentals=heads * rows * rows

time: 29.9 us -> 28.8 us (0.963)
  the two profiles are of different devices: /device:TPU:31 before, /device:TPU:21 now
where the time goes in v3:
time: 28.8 us; the launch traced here: 28.6 us
  Pallas kernels  26.4 us (92%)
  local copies, waits for them, and re-layouts  2.19 us (8%)
    pallas_call x1, Pallas kernels, per_device(): pl.pallas_call(functools.partial(kernel, seq_size, heads, rows, shard * s...  26.4 us
    unnamed x9, local copies, waits for them, and re-layouts  2.19 us

profile of v3, /device:TPU:21, one launch (start us, length us, event | category | flops | bytes accessed | tf_op | source)
XLA Modules:
  0.0 28.6 jit_solution(17705564177464741054)
XLA Ops:
  0.0 0.0 copy-start.3
  0.0 0.0 copy-start.2
  0.0 0.0 copy-start.1
  0.0 0.6 %copy-done.3 = f32[8]{0:T(128)S(1)} copy-done((f32[8]{0:T(128)S(1)}, f32[8]{0:T(128)}, u32[]{:S(2)}) %copy-start.3) | copy-done | bytes 56
  0.7 0.0 copy-done.2
  0.7 0.0 copy-done.1
  0.7 0.0 copy-start
  0.7 0.7 %copy-done = s32[512,8]{0,1:T(8,128)S(1)} copy-done((s32[512,8]{0,1:T(8,128)S(1)}, s32[512,8]{0,1:T(8,128)}, u32[]{:S(2)}) %copy-start) | copy-done | bytes 16408
  1.4 26.4 %shard_map.73 = bf16[256,1024]{1,0:T(8,128)(2,1)S(1)} custom-call(s32[3]{0:T(128)S(1)} %copy-done.1, f32[8]{0:T(128)S(1)} %copy-done.2, f32[8]{0:T(128)S(1)} %copy-done.3, bf16[256,1024]{1,0:T(8,128)(2,1)} %q_hbm.1, bf16[512,1024]{1,0:T(8,128)(2,1)} %k_hbm.1, bf16[512,1024]{1,0:T(8,128)(2,1)} %v_hbm.1, s32[8,512]{1,0:T(8,128)S(1)} %bitcast.1), custom_call_target="tpu_custom_call" | custom-call | flops 4026531840 | bytes 4194304 | tf_op jit(solution)/shard_map/pallas_call | solution.py:430
  27.8 0.8 %copy.9 = bf16[256,1024]{1,0:T(8,128)(2,1)} copy(bf16[256,1024]{1,0:T(8,128)(2,1)S(1)} %shard_map.73) | data formatting | bytes 1048576
Async XLA Ops:
  0.0 0.7 %copy-start.3 = (f32[8]{0:T(128)S(1)}, f32[8]{0:T(128)}, u32[]{:S(2)}) copy-start(f32[8]{0:T(128)} %ridge_ref.1) | copy-start | bytes 100
  0.0 0.7 %copy-start.2 = (f32[8]{0:T(128)S(1)}, f32[8]{0:T(128)}, u32[]{:S(2)}) copy-start(f32[8]{0:T(128)} %rates_ref.1) | copy-start | bytes 100
  0.0 0.7 %copy-start.1 = (s32[3]{0:T(128)S(1)}, s32[3]{0:T(128)}, u32[]{:S(2)}) copy-start(s32[3]{0:T(128)} %lengths_ref.1) | copy-start | bytes 40
  0.7 0.7 %copy-start = (s32[512,8]{0,1:T(8,128)S(1)}, s32[512,8]{0,1:T(8,128)}, u32[]{:S(2)}) copy-start(s32[512,8]{0,1:T(8,128)} %param.10) | copy-start | bytes 49156
